TPU v7x, 256 devices: a whole 4x4x8 slice. The times are simulated.
256 devices in a mesh: dp: 32 (over x, y, core), tensor: 8 (over z).
Axes of the slice: x: 4, y: 4, z: 8, core: 2. Of those that a mesh axis runs over, the one named last changes fastest.
Arguments:
- grad_key: float32 [32, 4096, 1024], P('dp', None, 'tensor'), as said below
- grad_value: float32 [32, 4096, 1024], P('dp', None, 'tensor'), as said below
- error_key: float32 [32, 4096, 1024], P('dp', None, 'tensor'), may hold values from -3 to 3
- error_value: float32 [32, 4096, 1024], P('dp', None, 'tensor'), may hold values from -3 to 3
- factor_key: float32 [1024, 32], P('tensor'), may hold values from -6 to 6
- factor_value: float32 [1024, 32], P('tensor'), may hold values from -6 to 6
Outputs:
- factor_key_new: float32 [1024, 32], P('tensor')
- factor_value_new: float32 [1024, 32], P('tensor')
- error_key_new: float32 [32, 4096, 1024], P('dp', None, 'tensor')
- error_value_new: float32 [32, 4096, 1024], P('dp', None, 'tensor')
Inputs may be any that keep to these rules, and one draw needn't show every extreme that they name: `grad_key`: float32 gradients of order one to some tens. `grad_value`: float32 gradients of order one to some tens.
All inputs are finite; a program needn't handle non-finite values.
Results may differ from a plain program's by a relative error of at most 0.0001.
Values sent between devices are 32-bit elements; how exact they have to be, the bound alone decides.
A program may use at most 64 MiB of HBM per device.

v0:
```python
import jax
import jax.numpy as jnp
from jax import lax
from jax.sharding import PartitionSpec as P


def orthonormal(left_factor, gram_matrix):
    lower_factor = jnp.linalg.cholesky(gram_matrix)
    return lax.linalg.triangular_solve(
        lower_factor, left_factor, left_side=False, lower=True, transpose_a=True
    )


def on_device(grad_key, grad_value, error_key, error_value, factor_key, factor_value):
    highest = lax.Precision.HIGHEST
    matrix_key = grad_key[0] + error_key[0]
    matrix_value = grad_value[0] + error_value[0]
    left_key = jnp.dot(matrix_key, factor_key, precision=highest)
    left_value = jnp.dot(matrix_value, factor_value, precision=highest)
    left_key, left_value = lax.psum((left_key, left_value), ("dp", "tensor"))
    basis_key = orthonormal(left_key, jnp.dot(left_key.T, left_key, precision=highest))
    basis_value = orthonormal(left_value, jnp.dot(left_value.T, left_value, precision=highest))
    right_key = jnp.dot(matrix_key.T, basis_key, precision=highest)
    right_value = jnp.dot(matrix_value.T, basis_value, precision=highest)
    right_key, right_value = lax.psum((right_key, right_value), "dp")
    replicas = lax.axis_size("dp")
    right_key = right_key / replicas
    right_value = right_value / replicas
    new_key = matrix_key - jnp.dot(basis_key, right_key.T, precision=highest)
    new_value = matrix_value - jnp.dot(basis_value, right_value.T, precision=highest)
    return (right_key, right_value, new_key[None], new_value[None])


def solution(mesh):
    in_specs = (
        P("dp", None, "tensor"),
        P("dp", None, "tensor"),
        P("dp", None, "tensor"),
        P("dp", None, "tensor"),
        P("tensor", None),
        P("tensor", None),
    )
    out_specs = (
        P("tensor", None),
        P("tensor", None),
        P("dp", None, "tensor"),
        P("dp", None, "tensor"),
    )
    return jax.shard_map(
        on_device, mesh=mesh, in_specs=in_specs, out_specs=out_specs, check_vma=False
    )
```

profile of v0, /device:TPU:1, one launch (start us, length us, event | category | flops | bytes accessed | tf_op | source)
XLA Modules:
  0.0 441.7 jit_solution(11683274292722043017)
XLA Ops:
  7.2 0.0 copy-start
  7.2 0.0 copy-start.1
  7.2 0.0 copy-start.11
  7.2 0.0 all-reduce.4.cloned.1.call-start
  7.2 0.6 copy-done
  7.9 0.0 copy-start.2
  7.9 5.4 %fusion.8 = f32[4096,32]{0,1:T(8,128)} fusion(f32[128,32]{0,1:T(8,128)S(1)} %copy-done, f32[1,4096,128]{2,1,0:T(8,128)} %param.9, f32[1,4096,128]{2,1,0:T(8,128)} %param.11), kind=kOutput, calls=%fused_computation.12 | convolution fusion | flops 201850880 | bytes 4734976 | tf_op jit(solution)/shard_map/dot_general | solution.py:18
  13.3 0.0 copy-done.1
  13.3 0.0 copy-done.11
  13.3 0.0 copy-done.2
  13.3 3.1 fusion.4
  16.3 0.0 all-reduce.4.cloned.1.call-update
  16.4 258.7 %all-reduce.4.cloned.1.call-done = (f32[4096,32]{0,1:T(8,128)}, f32[4096,32]{0,1:T(8,128)}) async-done(((f32[4096,32]{0,1:T(8,128)}, f32[4096,32]{0,1:T(8,128)}), (f32[4096,32]{0,1:T(8,128)}, f32[4096,32]{0,1:T(8,128)})) %all-reduce.4.cloned.1.call-update) | async-done | bytes 1048592 | tf_op jit(solution)/shard_map/psum | solution.py:20
  275.0 0.0 copy-start.6
  275.0 1.8 fusion.20
  276.9 1.8 fusion.21
  278.6 0.1 copy.11
  278.7 2.9 cholesky.55
  281.7 0.6 compare_reduce_fusion
  282.3 0.7 fusion.11
  283.0 2.4 custom-call.7
  285.4 0.0 copy-done.6
  285.4 0.7 convolution_bitcast_fusion
  286.1 0.0 copy-start.5
  286.1 3.0 fusion.2
  289.1 0.1 copy.10
  289.2 2.9 cholesky.44
  292.1 0.6 compare_reduce_fusion.1
  292.8 0.7 fusion.10
  293.4 2.4 custom-call.6
  295.9 0.0 copy-done.5
  295.9 0.7 convolution_bitcast_fusion.1
  296.5 0.0 copy-start.7
  296.5 0.8 copy-done.7
  297.3 3.6 fusion.6
  300.9 123.1 %all-reduce.1 = (f32[128,32]{0,1:T(8,128)S(1)}, f32[128,32]{0,1:T(8,128)S(1)}) all-reduce(f32[128,32]{0,1:T(8,128)S(1)} %fusion.6, f32[128,32]{0,1:T(8,128)S(1)} %fusion.2), channel_id=1, replica_groups=mesh['dp'=32,'tensor'=8] {'dp'}, use_global_device_ids=true, to_apply=%region_3.6 | all-reduce | flops 8192 | bytes 65536 | tf_op jit(solution)/shard_map/psum | solution.py:25
  424.0 0.0 copy-start.9
  424.0 0.0 copy-start.10
  424.0 0.0 copy-start.3
  424.0 0.0 copy-start.4
  424.0 0.0 copy-start.8
  424.0 6.0 %fusion = f32[1,4096,128]{2,1,0:T(8,128)} fusion(f32[4096,32]{0,1:T(8,128)S(1)} %convolution_bitcast_fusion, f32[128,32]{0,1:T(8,128)S(1)} %get-tuple-element.10, f32[1,4096,128]{2,1,0:T(8,128)S(1)} %copy-done.1, f32[1,4096,128]{2,1,0:T(8,128)} %param.12), kind=kOutput, calls=%fused_computation.1 | convolution fusion | flops 202375168 | bytes 6832128 | tf_op jit(solution)/shard_map/dot_general | solution.py:30
  430.0 0.0 copy-done.9
  430.0 0.0 copy-done.10
  430.0 0.0 copy-done.3
  430.0 0.0 copy-done.4
  430.0 0.0 copy-done.8
  430.1 4.8 %fusion.1 = f32[1,4096,128]{2,1,0:T(8,128)} fusion(f32[4096,32]{0,1:T(8,128)S(1)} %copy-done.8, f32[128,32]{0,1:T(8,128)S(1)} %get-tuple-element.11, f32[1,4096,128]{2,1,0:T(8,128)S(1)} %copy-done.3, f32[1,4096,128]{2,1,0:T(8,128)S(1)} %copy-done.4), kind=kOutput, calls=%fused_computation.3 | convolution fusion | flops 202375168 | bytes 6832128 | tf_op jit(solution)/shard_map/dot_general | solution.py:29
  (5 shorter events, 0.1 us)
Async XLA Ops:
  7.2 0.7 copy-start
  7.2 6.1 %copy-start.1 = (f32[1,4096,128]{2,1,0:T(8,128)S(1)}, f32[1,4096,128]{2,1,0:T(8,128)}, u32[]{:S(2)}) copy-start(f32[1,4096,128]{2,1,0:T(8,128)} %param.10) | copy-start | bytes 6291460
  7.2 6.1 %copy-start.11 = (f32[128,32]{0,1:T(8,128)S(1)}, f32[128,32]{0,1:T(8,128)}, u32[]{:S(2)}) copy-start(f32[128,32]{0,1:T(8,128)} %param.14) | copy-start | bytes 49156
  7.2 267.8 %all-reduce.4.cloned.1.call-start = ((), (), s32[]{:S(2)}) async-start(), calls=%async_computation | async-start | bytes 2097152 | tf_op jit(solution)/shard_map/psum | solution.py:20
  7.9 5.4 %copy-start.2 = (f32[1,4096,128]{2,1,0:T(8,128)S(1)}, f32[1,4096,128]{2,1,0:T(8,128)}, u32[]{:S(2)}) copy-start(f32[1,4096,128]{2,1,0:T(8,128)} %param.12) | copy-start | bytes 6291460
  275.0 10.4 %copy-start.6 = (f32[4096,32]{0,1:T(8,128)S(1)}, f32[4096,32]{0,1:T(8,128)}, u32[]{:S(2)}) copy-start(f32[4096,32]{0,1:T(8,128)} %get-tuple-element.7) | copy-start | bytes 1572868
  286.1 9.8 %copy-start.5 = (f32[4096,32]{0,1:T(8,128)S(1)}, f32[4096,32]{0,1:T(8,128)}, u32[]{:S(2)}) copy-start(f32[4096,32]{0,1:T(8,128)} %get-tuple-element.6) | copy-start | bytes 1572868
  296.5 0.8 copy-start.7
  424.0 6.0 %copy-start.9 = (f32[128,32]{0,1:T(8,128)}, f32[128,32]{0,1:T(8,128)S(1)}, u32[]{:S(2)}) copy-start(f32[128,32]{0,1:T(8,128)S(1)} %get-tuple-element.10) | copy-start | bytes 49156
  424.0 6.0 %copy-start.10 = (f32[128,32]{0,1:T(8,128)}, f32[128,32]{0,1:T(8,128)S(1)}, u32[]{:S(2)}) copy-start(f32[128,32]{0,1:T(8,128)S(1)} %get-tuple-element.11) | copy-start | bytes 49156
  424.0 6.0 %copy-start.3 = (f32[1,4096,128]{2,1,0:T(8,128)S(1)}, f32[1,4096,128]{2,1,0:T(8,128)}, u32[]{:S(2)}) copy-start(f32[1,4096,128]{2,1,0:T(8,128)} %param.9) | copy-start | bytes 6291460
  424.0 6.0 %copy-start.4 = (f32[1,4096,128]{2,1,0:T(8,128)S(1)}, f32[1,4096,128]{2,1,0:T(8,128)}, u32[]{:S(2)}) copy-start(f32[1,4096,128]{2,1,0:T(8,128)} %param.11) | copy-start | bytes 6291460
  424.0 6.0 %copy-start.8 = (f32[4096,32]{0,1:T(8,128)S(1)}, f32[4096,32]{0,1:T(8,128)}, u32[]{:S(2)}) copy-start(f32[4096,32]{0,1:T(8,128)} %copy-done.7) | copy-start | bytes 1572868
Sparse Core Ops, SparseCore 0:
  16.5 258.5 all-reduce.3
where the time goes:
time: 446 us; the launch traced here: 442 us
  waiting for transfers between devices  259 us (58%)
  blocking collectives  123 us (28%)
  matrix products  30.7 us (7%)
  between operations  14.2 us (3%)
  other arithmetic  13.4 us (3%)
    psum x1, waiting for transfers between devices, on_device(): left_key, left_value = lax.psum((left_key, left_value), ('dp', 'tensor'))  259 us
    psum x1, blocking collectives, on_device(): right_key, right_value = lax.psum((right_key, right_value), 'dp')  123 us
  transfers between devices with their start and end apart: 1, of which 1 were waited for; matrix products, arithmetic and copies ran while one was open for 0% of the time, Pallas kernels for 0%

commit v1 on v0

v1 whole, which is shorter than its diff:
```python
import functools

import jax
import jax.numpy as jnp
from jax import lax
from jax.experimental import pallas as pl
from jax.experimental.pallas import tpu as pltpu
from jax.sharding import PartitionSpec as P

MESH = pl.DeviceIdType.MESH
F32 = jnp.float32
BF16 = jnp.bfloat16
D = 4096
F = 128
RANK = 32
SUPERS = 8
ROWS = D // SUPERS
SUB = ROWS // 128
CHIPS = 32
PLANE = 16
QUADS = 4


def nt(a, b):
    return lax.dot_general(a, b, (((1,), (1,)), ((), ())), preferred_element_type=F32)


def nn(a, b):
    return jnp.dot(a, b, preferred_element_type=F32)


def full(a, b):
    return jnp.dot(a, b, preferred_element_type=F32, precision=lax.Precision.HIGHEST)


def split(value):
    high = value.astype(BF16)
    return high, (value - high.astype(F32)).astype(BF16)


def reduce_kernel(
    gk, gv, ek, ev, qk, qv,
    fed, left_rows, weight, right,
    stage, fed_high, fed_low, q_all, part, pair_in, ring_in, quad_in, left, acc_high, acc_low,
    t_part, t_pair, t_plane, t_sum,
    load_sem, pair_send, pair_recv, ring_send, ring_recv, quad_send, quad_recv,
    gather_send, gather_recv, pass_send, pass_recv, t_send, t_recv,
):
    dp = lax.axis_index("dp")
    z = lax.axis_index("tensor")
    core = dp % 2
    chip = dp // 2
    x = chip // 4
    y = chip % 4
    bit = z % 2
    quad = z // 2
    me = chip * 2 + bit
    base = me // SUB
    partner = (chip * 2 + 1 - core, z)

    def chip_of(member):
        return ((member // 2) * 2 + core, quad * 2 + member % 2)

    def member_at(offset):
        return (((x + offset // 8) % 4) * 4 + (y + (offset // 2) % 4) % 4) * 2 + (bit + offset % 2) % 2

    def block(step):
        return (base + 2 + step) % SUPERS

    def load(step, a, ref):
        rows = pl.ds(pl.multiple_of(block(step) * ROWS, ROWS), ROWS)
        return pltpu.make_async_copy(ref.at[0, rows], stage.at[a, rows], load_sem.at[step, a])

    def start_load(step, carry):
        for a, ref in enumerate((gk, gv, ek, ev)):
            load(step, a, ref).start()
        return carry

    lax.fori_loop(0, SUPERS, start_load, 0)

    barrier = pltpu.get_barrier_semaphore()

    def greet(i, carry):
        pl.semaphore_signal(barrier, inc=1, device_id=chip_of(member_at(i)), device_id_type=MESH)
        return carry

    lax.fori_loop(1, CHIPS, greet, 0)
    for i in range(1, QUADS):
        pl.semaphore_signal(barrier, inc=1, device_id=(dp, ((quad + i) % QUADS) * 2 + bit), device_id_type=MESH)
    pl.semaphore_signal(barrier, inc=1, device_id=partner, device_id_type=MESH)

    q_all[...] = jnp.zeros_like(q_all)
    for m, q in enumerate((qk, qv)):
        for part_of, piece in enumerate(split(q[...])):
            row = part_of * 2 * RANK + m * RANK
            q_all[row : row + RANK, m * F : (m + 1) * F] = piece

    def add_left(step, carry):
        b = block(step)
        rows = pl.ds(pl.multiple_of(b * ROWS, ROWS), ROWS)
        for a, ref in enumerate((gk, gv, ek, ev)):
            load(step, a, ref).wait()
        highs, lows = [], []
        for m in range(2):
            value = stage[m, rows, :] + stage[2 + m, rows, :]
            fed[rows, m * F : (m + 1) * F] = value
            high, low = split(value)
            fed_high[rows, m * F : (m + 1) * F] = high
            fed_low[rows, m * F : (m + 1) * F] = low
            highs.append(high)
            lows.append(low)
        high = jnp.concatenate(highs, axis=1)
        low = jnp.concatenate(lows, axis=1)
        product = nt(q_all[...], high)
        total = product[: 2 * RANK] + product[2 * RANK :] + nt(q_all[: 2 * RANK, :], low)
        for m in range(2):
            for j in range(SUB):
                part[m, b * SUB + j] = total[m * RANK : (m + 1) * RANK, j * 128 : (j + 1) * 128]
        return carry

    lax.fori_loop(0, SUPERS, add_left, 0)
    pl.semaphore_wait(barrier, CHIPS - 1 + QUADS - 1 + 1)

    def pair_copy(step):
        at = pl.ds(block(step) * SUB, SUB)
        return pltpu.make_async_remote_copy(
            src_ref=part.at[1 - core, at], dst_ref=pair_in.at[at], send_sem=pair_send.at[step],
            recv_sem=pair_recv.at[step], device_id=partner, device_id_type=MESH)

    def start_pair(step, carry):
        pair_copy(step).start()
        return carry

    lax.fori_loop(0, SUPERS, start_pair, 0)

    def ring_copy(member):
        return pltpu.make_async_remote_copy(
            src_ref=part.at[core, member], dst_ref=ring_in.at[me], send_sem=ring_send,
            recv_sem=ring_recv, device_id=chip_of(member), device_id_type=MESH)

    def scatter(step, carry):
        pair_copy(step).wait_recv()
        b = block(step)
        for j in range(SUB):
            member = b * SUB + j
            part[core, member] = part[core, member] + pair_in[member]

            @pl.when(member != me)
            def _():
                ring_copy(member).start()
        return carry

    lax.fori_loop(0, SUPERS, scatter, 0)
    ring_in[me] = part[core, me]
    most = pl.ds(0, CHIPS - 1)
    pltpu.make_async_copy(ring_in.at[most], ring_in.at[most], ring_recv).wait()
    quad_in[quad] = jnp.sum(ring_in[...], axis=0)

    def quad_copy(i):
        return pltpu.make_async_remote_copy(
            src_ref=quad_in.at[quad], dst_ref=quad_in.at[quad], send_sem=quad_send, recv_sem=quad_recv,
            device_id=(dp, ((quad + i) % QUADS) * 2 + bit), device_id_type=MESH)

    for i in (2, 1, 3):
        quad_copy(i).start()
    three = pl.ds(0, QUADS - 1)
    pltpu.make_async_copy(quad_in.at[three], quad_in.at[three], quad_recv).wait()
    left[core, me] = (quad_in[0] + quad_in[1]) + (quad_in[2] + quad_in[3])

    def gather_copy(member, slot):
        return pltpu.make_async_remote_copy(
            src_ref=left.at[core, slot], dst_ref=left.at[core, slot], send_sem=gather_send,
            recv_sem=gather_recv.at[slot], device_id=chip_of(member), device_id_type=MESH)

    def pass_copy(slot):
        return pltpu.make_async_remote_copy(
            src_ref=left.at[core, slot], dst_ref=left.at[core, slot], send_sem=pass_send,
            recv_sem=pass_recv.at[slot], device_id=partner, device_id_type=MESH)

    def start_gather(i, carry):
        offset = (i + CHIPS // 2) % CHIPS

        @pl.when(offset != 0)
        def _():
            gather_copy(member_at(offset), me).start()
        return carry

    lax.fori_loop(0, CHIPS, start_gather, 0)
    pass_copy(me).start()

    def near(step):
        turn = step // 2
        dx = turn + (turn // 2) * (1 - 2 * (turn % 2))
        return ((x + dx) % 4) * 2 + (base + step) % 2

    def forward(step):
        for j in range(SUB):
            slot = near(step) * SUB + j

            @pl.when(slot != me)
            def _():
                gather_copy(me, slot).wait_recv()
                pass_copy(slot).start()

    def left_block(b):
        sides = []
        for m in range(2):
            sides.append(jnp.concatenate([left[m, b * SUB + j] for j in range(SUB)], axis=1))
        return jnp.concatenate(sides, axis=0)

    def add_right(step):
        b = near(step)
        for j in range(SUB):
            slot = b * SUB + j
            pltpu.make_async_remote_copy(
                src_ref=left.at[1 - core, slot], dst_ref=left.at[1 - core, slot], send_sem=pass_send,
                recv_sem=pass_recv.at[slot], device_id=partner, device_id_type=MESH).wait_recv()
        rows = pl.ds(pl.multiple_of(b * ROWS, ROWS), ROWS)
        high, low = split(left_block(b))
        acc_high[...] += nn(jnp.concatenate([high, low], axis=0), fed_high[rows, :])
        acc_low[...] += nn(high, fed_low[rows, :])

    acc_high[...] = jnp.zeros_like(acc_high)
    acc_low[...] = jnp.zeros_like(acc_low)
    forward(0)

    def gather_step(step, carry):
        forward(step)
        add_right(step - 1)
        return carry

    lax.fori_loop(1, SUPERS, gather_step, 0)
    add_right(SUPERS - 1)
    for m in range(2):
        r, s = slice(m * RANK, (m + 1) * RANK), slice((m + 2) * RANK, (m + 3) * RANK)
        f = slice(m * F, (m + 1) * F)
        t_part[m] = acc_high[r, f] + acc_high[s, f] + acc_low[r, f]

    t_first = pltpu.make_async_remote_copy(
        src_ref=t_part.at[1 - core], dst_ref=t_pair, send_sem=t_send.at[0], recv_sem=t_recv.at[0],
        device_id=partner, device_id_type=MESH)
    t_first.start()

    def gram_step(b, total):
        high, low = split(left_block(b))
        both = jnp.concatenate([high, low], axis=0)
        return total + nt(both, both)

    t_first.wait_recv()
    t_plane[chip] = t_part[core] + t_pair[...]

    def plane_copy(i):
        other = ((x + i // 4) % 4) * 4 + (y + i % 4) % 4
        return pltpu.make_async_remote_copy(
            src_ref=t_plane.at[chip], dst_ref=t_plane.at[chip], send_sem=t_send.at[1], recv_sem=t_recv.at[1],
            device_id=(other * 2 + core, z), device_id_type=MESH)

    def start_plane(i, carry):
        offset = (i + PLANE // 2) % PLANE

        @pl.when(offset != 0)
        def _():
            plane_copy(offset).start()
        return carry

    lax.fori_loop(0, PLANE, start_plane, 0)

    products = lax.fori_loop(0, SUPERS, gram_step, jnp.zeros((4 * RANK, 4 * RANK), F32))
    top, bottom = products[: 2 * RANK], products[2 * RANK :]
    gram = top[:, : 2 * RANK] + top[:, 2 * RANK :] + bottom[:, : 2 * RANK] + bottom[:, 2 * RANK :]
    row = lax.broadcasted_iota(jnp.int32, (RANK, RANK), 0)
    column = lax.broadcasted_iota(jnp.int32, (RANK, RANK), 1)
    unit = jnp.where(row == column, 1.0, 0.0).astype(F32)
    work = jnp.concatenate([gram[:RANK, :RANK], unit, gram[RANK:, RANK:], unit], axis=1)
    wide_row = lax.broadcasted_iota(jnp.int32, (RANK, 4 * RANK), 0)
    wide_column = lax.broadcasted_iota(jnp.int32, (RANK, 4 * RANK), 1)
    first = wide_column < 2 * RANK
    pivots = jnp.ones((RANK, 4 * RANK), F32)
    for j in range(RANK):
        picked = jnp.where(first, work[:, j : j + 1], work[:, 2 * RANK + j : 2 * RANK + j + 1])
        pivot = picked[j : j + 1, :]
        pivots = jnp.where(wide_row == j, pivot, pivots)
        work = work - jnp.where(wide_row > j, picked / pivot, 0.0) * work[j : j + 1, :]
    inverse = work * lax.rsqrt(pivots)
    key_inverse = jnp.where((wide_column >= RANK) & first, inverse, 0.0)
    value_inverse = jnp.where(wide_column >= 3 * RANK, inverse, 0.0)
    lower = jnp.concatenate([key_inverse, value_inverse, jnp.zeros((2 * RANK, 4 * RANK), F32)], axis=0)
    upper = lower.T

    def turn_step(b, carry):
        for m in range(SUB):
            slot = b * SUB + m
            value = jnp.concatenate([left[0, slot], left[1, slot]], axis=0)
            high, low = split(value)
            both = jnp.concatenate([high.astype(F32), low.astype(F32)], axis=0)
            left_rows[pl.ds(pl.multiple_of(slot * 128, 128), 128), :] = both.T.astype(BF16)
        return carry

    lax.fori_loop(0, SUPERS, turn_step, 0)

    fifteen = pl.ds(0, PLANE - 1)
    pltpu.make_async_copy(t_plane.at[fifteen], t_plane.at[fifteen], t_recv.at[1]).wait()
    t_sum[core] = jnp.sum(t_plane[...], axis=0)
    t_last = pltpu.make_async_remote_copy(
        src_ref=t_sum.at[core], dst_ref=t_sum.at[core], send_sem=t_send.at[2], recv_sem=t_recv.at[2],
        device_id=partner, device_id_type=MESH)
    t_last.start()
    t_last.wait_recv()
    none = jnp.zeros((RANK, F), F32)
    sums = jnp.concatenate([none, t_sum[0], none, t_sum[1]], axis=0) * (1.0 / 32)
    right_rows = full(lower, sums)
    solved = full(upper, right_rows)
    right[...] = right_rows[: 2 * RANK]
    weight[: RANK, :] = solved[RANK : 2 * RANK]
    weight[RANK:, :] = solved[3 * RANK :]

    def end_pair(step, carry):
        pair_copy(step).wait_send()
        return carry

    lax.fori_loop(0, SUPERS, end_pair, 0)
    pltpu.make_async_copy(ring_in.at[most], ring_in.at[most], ring_send).wait()
    pltpu.make_async_copy(quad_in.at[three], quad_in.at[three], quad_send).wait()
    pltpu.make_async_copy(ring_in.at[most], ring_in.at[most], gather_send).wait()
    pltpu.make_async_copy(ring_in, ring_in, pass_send).wait()
    t_first.wait_send()
    pltpu.make_async_copy(t_plane.at[fifteen], t_plane.at[fifteen], t_send.at[1]).wait()
    t_last.wait_send()


def error_kernel(fed, left_rows, weight, right, right_key, right_value, new_key, new_value, wide, out, sem):
    right_key[...] = right[:RANK]
    right_value[...] = right[RANK:]
    wide[...] = jnp.zeros_like(wide)
    for part_of, piece in enumerate(split(weight[...])):
        for again in range(2):
            row = (2 * part_of + again) * 2 * RANK
            wide[row : row + RANK, :F] = piece[:RANK]
            wide[row + RANK : row + 2 * RANK, F:] = piece[RANK:]
    copies = []
    for b in range(SUPERS):
        rows = slice(b * ROWS, (b + 1) * ROWS)
        tall = left_rows[rows, :]
        change = nn(jnp.concatenate([tall, tall], axis=1), wide[...])
        for m, new in enumerate((new_key, new_value)):
            out[m, rows, :] = fed[rows, m * F : (m + 1) * F] - change[:, m * F : (m + 1) * F]
            copy = pltpu.make_async_copy(out.at[m, rows], new.at[0, rows], sem.at[b, m])
            copy.start()
            copies.append(copy)
    for copy in copies:
        copy.wait()


def on_device(grad_key, grad_value, error_key, error_value, factor_key, factor_value):
    vmem = pl.BlockSpec(memory_space=pltpu.VMEM)
    anywhere = pl.BlockSpec(memory_space=pl.ANY)
    dma = pltpu.SemaphoreType.DMA
    fed, left_rows, weight, right = pl.pallas_call(
        reduce_kernel,
        out_shape=(
            jax.ShapeDtypeStruct((D, 2 * F), F32),
            jax.ShapeDtypeStruct((D, 4 * RANK), BF16),
            jax.ShapeDtypeStruct((2 * RANK, F), F32),
            jax.ShapeDtypeStruct((2 * RANK, F), F32),
        ),
        in_specs=[pl.BlockSpec(memory_space=pltpu.HBM)] * 4 + [vmem] * 2,
        out_specs=(vmem,) * 4,
        scratch_shapes=[
            pltpu.VMEM((4, D, F), F32),
            pltpu.VMEM((D, 2 * F), BF16),
            pltpu.VMEM((D, 2 * F), BF16),
            pltpu.VMEM((4 * RANK, 2 * F), BF16),
            pltpu.VMEM((2, CHIPS, RANK, 128), F32),
            pltpu.VMEM((CHIPS, RANK, 128), F32),
            pltpu.VMEM((CHIPS, RANK, 128), F32),
            pltpu.VMEM((QUADS, RANK, 128), F32),
            pltpu.VMEM((2, CHIPS, RANK, 128), F32),
            pltpu.VMEM((4 * RANK, 2 * F), F32),
            pltpu.VMEM((2 * RANK, 2 * F), F32),
            pltpu.VMEM((2, RANK, F), F32),
            pltpu.VMEM((RANK, F), F32),
            pltpu.VMEM((PLANE, RANK, F), F32),
            pltpu.VMEM((2, RANK, F), F32),
            dma((SUPERS, 4)),
            dma((SUPERS,)),
            dma((SUPERS,)),
            dma,
            dma,
            dma,
            dma,
            dma,
            dma((CHIPS,)),
            dma,
            dma((CHIPS,)),
            dma((3,)),
            dma((3,)),
        ],
        compiler_params=pltpu.CompilerParams(
            collective_id=0, has_side_effects=True, vmem_limit_bytes=32 * 2**20
        ),
        cost_estimate=pl.CostEstimate(flops=10**9, bytes_accessed=12 * 2**20, transcendentals=0),
        name="reduce_factors",
    )(grad_key, grad_value, error_key, error_value, factor_key.T, factor_value.T)
    right_key, right_value, new_key, new_value = pl.pallas_call(
        error_kernel,
        out_shape=(
            jax.ShapeDtypeStruct((RANK, F), F32),
            jax.ShapeDtypeStruct((RANK, F), F32),
            jax.ShapeDtypeStruct((1, D, F), F32),
            jax.ShapeDtypeStruct((1, D, F), F32),
        ),
        in_specs=[vmem] * 4,
        out_specs=(vmem, vmem, anywhere, anywhere),
        scratch_shapes=[
            pltpu.VMEM((8 * RANK, 2 * F), BF16),
            pltpu.VMEM((2, D, F), F32),
            dma((SUPERS, 2)),
        ],
        compiler_params=pltpu.CompilerParams(vmem_limit_bytes=32 * 2**20),
        cost_estimate=pl.CostEstimate(flops=10**9, bytes_accessed=8 * 2**20, transcendentals=0),
        name="new_errors",
    )(fed, left_rows, weight, right)
    return right_key.T, right_value.T, new_key, new_value


def solution(mesh):
    in_specs = (
        P("dp", None, "tensor"),
        P("dp", None, "tensor"),
        P("dp", None, "tensor"),
        P("dp", None, "tensor"),
        P("tensor", None),
        P("tensor", None),
    )
    out_specs = (
        P("tensor", None),
        P("tensor", None),
        P("dp", None, "tensor"),
        P("dp", None, "tensor"),
    )
    return jax.shard_map(
        on_device, mesh=mesh, in_specs=in_specs, out_specs=out_specs, check_vma=False
    )
```

time: 446 us -> 63 us (0.14)
  waiting for transfers between devices: 259 us -> 0 us
  blocking collectives: 123 us -> 0 us
  Pallas kernels: 0 us -> 54.2 us
  matrix products: 30.7 us -> 0 us
  between operations: 14.2 us -> 0.65 us
  other arithmetic: 13.4 us -> 0 us
  local copies, waits for them, and re-layouts: 1.63 us -> 7.79 us
    psum x1 -> x0, waiting for transfers between devices: 259 us -> none  [on_device(): left_key, left_value = lax.psum((left_key, left_value), ('dp', 'tensor'))]
    psum x1 -> x0, blocking collectives: 123 us -> none  [on_device(): right_key, right_value = lax.psum((right_key, right_value), 'dp')]
    pallas_call x0 -> x2, Pallas kernels: none -> 54.2 us  [the longest x1 51.2 us: on_device(): pl.pallas_call(reduce_kernel, out_shape=(jax.ShapeDtypeStruct((D, 2 * F),...]
    dot_general x8 -> x0, matrix products: 29.4 us -> none  [the longest x1 5.99 us: on_device(): jnp.dot(basis_value, right_value.T, precision=highest)]
    another operation x10 -> x0, other arithmetic: 13.4 us -> none  [the longest x6 7.19 us: orthonormal(): lower_factor = jnp.linalg.cholesky(gram_matrix)]
    unnamed x24 -> x12, local copies, waits for them, and re-layouts: 1.48 us -> 7.79 us
  transfers between devices with their start and end apart: 1 -> 0, of which waited for: 1 -> 0; matrix products, arithmetic and copies ran while one was open for 0% -> 0% of each run, Pallas kernels for 0% -> 0%
where the time goes in v1:
time: 63 us; the launch traced here: 62.7 us
  Pallas kernels  54.2 us (86%)
  local copies, waits for them, and re-layouts  7.79 us (12%)
  between operations  0.65 us (1%)
    pallas_call x1, Pallas kernels, on_device(): pl.pallas_call(reduce_kernel, out_shape=(jax.ShapeDtypeStruct((D, 2 * F),...  51.2 us
    unnamed x12, local copies, waits for them, and re-layouts  7.79 us
    pallas_call x1, Pallas kernels, on_device(): pl.pallas_call(error_kernel, out_shape=(jax.ShapeDtypeStruct((RANK, F), F...  3.07 us

profile of v1, /device:TPU:1, one launch (start us, length us, event | category | flops | bytes accessed | tf_op | source)
XLA Modules:
  0.0 62.7 jit_solution(15365625204269276250)
XLA Ops:
  0.6 0.0 copy-start
  0.6 1.6 %copy-done = f32[1,4096,128]{2,1,0:T(8,128)S(1)} copy-done((f32[1,4096,128]{2,1,0:T(8,128)S(1)}, f32[1,4096,128]{2,1,0:T(8,128)}, u32[]{:S(2)}) %copy-start) | copy-done | bytes 2097176
  2.2 0.0 copy-start.1
  2.2 1.6 %copy-done.1 = f32[1,4096,128]{2,1,0:T(8,128)S(1)} copy-done((f32[1,4096,128]{2,1,0:T(8,128)S(1)}, f32[1,4096,128]{2,1,0:T(8,128)}, u32[]{:S(2)}) %copy-start.1) | copy-done | bytes 2097176
  3.8 0.0 copy-start.2
  3.8 1.6 %copy-done.2 = f32[1,4096,128]{2,1,0:T(8,128)S(1)} copy-done((f32[1,4096,128]{2,1,0:T(8,128)S(1)}, f32[1,4096,128]{2,1,0:T(8,128)}, u32[]{:S(2)}) %copy-start.2) | copy-done | bytes 2097176
  5.4 0.0 copy-start.3
  5.4 1.6 %copy-done.3 = f32[1,4096,128]{2,1,0:T(8,128)S(1)} copy-done((f32[1,4096,128]{2,1,0:T(8,128)S(1)}, f32[1,4096,128]{2,1,0:T(8,128)}, u32[]{:S(2)}) %copy-start.3) | copy-done | bytes 2097176
  7.0 0.0 copy-start.4
  7.0 0.7 %copy-done.4 = f32[128,32]{0,1:T(8,128)S(1)} copy-done((f32[128,32]{0,1:T(8,128)S(1)}, f32[128,32]{0,1:T(8,128)}, u32[]{:S(2)}) %copy-start.4) | copy-done | bytes 16408
  7.7 0.0 copy-start.5
  7.7 0.7 %copy-done.5 = f32[128,32]{0,1:T(8,128)S(1)} copy-done((f32[128,32]{0,1:T(8,128)S(1)}, f32[128,32]{0,1:T(8,128)}, u32[]{:S(2)}) %copy-start.5) | copy-done | bytes 16408
  8.4 51.2 %reduce_factors.1 = (f32[4096,256]{1,0:T(8,128)S(1)}, bf16[4096,128]{1,0:T(8,128)(2,1)S(1)}, f32[64,128]{1,0:T(8,128)S(1)}, f32[64,128]{1,0:T(8,128)S(1)}) custom-call(f32[1,4096,128]{2,1,0:T(8,128)S(1)} %copy-done, f32[1,4096,128]{2,1,0:T(8,128)S(1)} %copy-done.1, f32[1,4096,128]{2,1,0:T(8,128)S(1)} %copy-done.2, f32[1,4096,128]{2,1,0:T(8,128)S(1)} %copy-done.3, ...), custom_call_target="tpu_custom_call" | custom-call | flops 1000000000 | bytes 12582912 | tf_op jit(solution)/shard_map/reduce_factors/pallas_call | solution.py:358
  59.6 3.1 %new_errors.1 = (f32[32,128]{1,0:T(8,128)}, f32[32,128]{1,0:T(8,128)}, f32[1,4096,128]{2,1,0:T(8,128)}, f32[1,4096,128]{2,1,0:T(8,128)}) custom-call(f32[4096,256]{1,0:T(8,128)S(1)} %get-tuple-element.12.fed, bf16[4096,128]{1,0:T(8,128)(2,1)S(1)} %get-tuple-element.13.left_rows, f32[64,128]{1,0:T(8,128)S(1)} %get-tuple-element.14.weight, ...), custom_call_target="tpu_custom_call" | custom-call | flops 1000000000 | bytes 8388608 | tf_op jit(solution)/shard_map/new_errors/pallas_call | solution.py:404
Async XLA Ops:
  0.6 1.6 %copy-start = (f32[1,4096,128]{2,1,0:T(8,128)S(1)}, f32[1,4096,128]{2,1,0:T(8,128)}, u32[]{:S(2)}) copy-start(f32[1,4096,128]{2,1,0:T(8,128)} %gk.1) | copy-start | bytes 6291460
  2.2 1.6 %copy-start.1 = (f32[1,4096,128]{2,1,0:T(8,128)S(1)}, f32[1,4096,128]{2,1,0:T(8,128)}, u32[]{:S(2)}) copy-start(f32[1,4096,128]{2,1,0:T(8,128)} %gv.1) | copy-start | bytes 6291460
  3.8 1.6 %copy-start.2 = (f32[1,4096,128]{2,1,0:T(8,128)S(1)}, f32[1,4096,128]{2,1,0:T(8,128)}, u32[]{:S(2)}) copy-start(f32[1,4096,128]{2,1,0:T(8,128)} %ek.1) | copy-start | bytes 6291460
  5.4 1.6 %copy-start.3 = (f32[1,4096,128]{2,1,0:T(8,128)S(1)}, f32[1,4096,128]{2,1,0:T(8,128)}, u32[]{:S(2)}) copy-start(f32[1,4096,128]{2,1,0:T(8,128)} %ev.1) | copy-start | bytes 6291460
  7.0 0.7 %copy-start.4 = (f32[128,32]{0,1:T(8,128)S(1)}, f32[128,32]{0,1:T(8,128)}, u32[]{:S(2)}) copy-start(f32[128,32]{0,1:T(8,128)} %param.10) | copy-start | bytes 49156
  7.7 0.7 %copy-start.5 = (f32[128,32]{0,1:T(8,128)S(1)}, f32[128,32]{0,1:T(8,128)}, u32[]{:S(2)}) copy-start(f32[128,32]{0,1:T(8,128)} %param.11) | copy-start | bytes 49156

commit v2 on v1

v2 whole, which is shorter than its diff:
```python
import functools

import jax
import jax.numpy as jnp
from jax import lax
from jax.experimental import pallas as pl
from jax.experimental.pallas import tpu as pltpu
from jax.sharding import PartitionSpec as P

MESH = pl.DeviceIdType.MESH
F32 = jnp.float32
BF16 = jnp.bfloat16
D = 4096
F = 128
RANK = 32
SUPERS = 8
ROWS = D // SUPERS
SUB = ROWS // 128
CHIPS = 32
PLANE = 16
QUADS = 4
OFFSETS = sorted(
    [(dx, dy, dz) for dx in range(4) for dy in range(4) for dz in range(2) if dx + dy + dz > 0],
    key=lambda o: -(min(o[0], 4 - o[0]) + min(o[1], 4 - o[1]) + o[2]),
)


def nt(a, b):
    return lax.dot_general(a, b, (((1,), (1,)), ((), ())), preferred_element_type=F32)


def nn(a, b):
    return jnp.dot(a, b, preferred_element_type=F32)


def full(a, b):
    return jnp.dot(a, b, preferred_element_type=F32, precision=lax.Precision.HIGHEST)


def split(value):
    high = value.astype(BF16)
    return high, (value - high.astype(F32)).astype(BF16)


def reduce_kernel(
    gk, gv, ek, ev, qk, qv,
    fed, left_rows, result,
    stage, q_in, q_all, part, pair_in, ring_in, quad_in, left, share_in, shared, acc, t_plane,
    q_sem, load_sem, pair_send, pair_recv, ring_send, ring_recv, share_send, share_recv, quad_send, quad_recv,
    gather_send, gather_recv, pass_send, pass_recv, plane_send, plane_recv, last_send, last_recv,
):
    dp = lax.axis_index("dp")
    z = lax.axis_index("tensor")
    core = dp & 1
    chip = dp >> 1
    x = chip >> 2
    y = chip & 3
    bit = z & 1
    quad = z >> 1
    me = chip * 2 + bit
    xs = [(x + i) & 3 for i in range(4)]
    ys = [(y + i) & 3 for i in range(4)]
    bits = [bit, 1 - bit]
    partner = (chip * 2 + 1 - core, z)
    quads = [(dp, ((quad + i) & 3) * 2 + bit) for i in range(QUADS)]

    def device_at(offset):
        dx, dy, dz = offset
        return ((xs[dx] * 4 + ys[dy]) * 2 + core, quad * 2 + bits[dz])

    def block(step):
        inner = (step >= 2) & (step < 6)
        dx = jnp.where(step < 2, 2, jnp.where(inner, 1 + 2 * (step & 1), 0))
        half = jnp.where(inner, 2 - (step >> 1), 1 - (step & 1))
        return ((x + dx) & 3) * 2 + (((y >> 1) + half) & 1)

    def rows_of(b):
        return pl.ds(pl.multiple_of(b * ROWS, ROWS), ROWS)

    def slots_of(b):
        return pl.ds(b * SUB, SUB)

    def load(step, a, ref):
        rows = rows_of(block(step))
        return pltpu.make_async_copy(ref.at[0, rows], stage.at[a, rows], load_sem.at[step, a])

    def start_load(step, carry):
        for a, ref in enumerate((gk, gv, ek, ev)):
            load(step, a, ref).start()
        return carry

    q_loads = [pltpu.make_async_copy(q, q_in.at[m], q_sem.at[m]) for m, q in enumerate((qk, qv))]
    for q_load in q_loads:
        q_load.start()
    lax.fori_loop(0, 2, start_load, 0)

    barrier = pltpu.get_barrier_semaphore()
    for target in [device_at(offset) for offset in OFFSETS] + quads[1:] + [partner]:
        pl.semaphore_signal(barrier, inc=1, device_id=target, device_id_type=MESH)
    lax.fori_loop(2, SUPERS, start_load, 0)

    q_all[...] = jnp.zeros_like(q_all)
    for m in range(2):
        q_loads[m].wait()
        for part_of, piece in enumerate(split(q_in[m])):
            row = part_of * 2 * RANK + m * RANK
            q_all[row : row + RANK, m * F : (m + 1) * F] = piece

    def add_left(step, carry):
        b = block(step)
        rows = rows_of(b)
        for a, ref in enumerate((gk, gv, ek, ev)):
            load(step, a, ref).wait()
        highs, lows = [], []
        for m in range(2):
            value = stage[m, rows, :] + stage[2 + m, rows, :]
            fed[m, rows, :] = value
            high, low = split(value)
            highs.append(high)
            lows.append(low)
        high = jnp.concatenate(highs, axis=1)
        low = jnp.concatenate(lows, axis=1)
        product = nt(q_all[...], high)
        total = product[: 2 * RANK] + product[2 * RANK :] + nt(q_all[: 2 * RANK, :], low)
        for m in range(2):
            for j in range(SUB):
                part[m, b * SUB + j] = total[m * RANK : (m + 1) * RANK, j * 128 : (j + 1) * 128]
        return carry

    lax.fori_loop(0, SUPERS, add_left, 0)
    pl.semaphore_wait(barrier, len(OFFSETS) + QUADS)

    def pair_copy(step):
        at = slots_of(block(step))
        return pltpu.make_async_remote_copy(
            src_ref=part.at[1 - core, at], dst_ref=pair_in.at[at], send_sem=pair_send.at[step],
            recv_sem=pair_recv.at[step], device_id=partner, device_id_type=MESH)

    def start_pair(step, carry):
        pair_copy(step).start()
        return carry

    lax.fori_loop(0, SUPERS, start_pair, 0)

    def ring_copy(member):
        target = ((member >> 1) * 2 + core, quad * 2 + (member & 1))
        return pltpu.make_async_remote_copy(
            src_ref=part.at[core, member], dst_ref=ring_in.at[me], send_sem=ring_send,
            recv_sem=ring_recv, device_id=target, device_id_type=MESH)

    def scatter(step, kept):
        pair_copy(step).wait_recv()
        b = block(step)
        at = slots_of(b)
        part[core, at] = part[core, at] + pair_in[at]
        for dy in (1, 0):
            for dz in (1, 0):
                if (dy, dz) != (0, 0) or not kept:
                    ring_copy(b * SUB + ((y + dy) & 1) * 2 + bits[dz]).start()

    def scatter_step(step, carry):
        scatter(step, False)
        return carry

    lax.fori_loop(0, SUPERS - 1, scatter_step, 0)
    scatter(SUPERS - 1, True)
    ring_in[me] = part[core, me]

    def share_copy(step):
        rows = rows_of(block(step))
        return pltpu.make_async_remote_copy(
            src_ref=fed.at[1 - core, rows], dst_ref=share_in.at[rows], send_sem=share_send.at[step],
            recv_sem=share_recv.at[step], device_id=partner, device_id_type=MESH)

    def start_share(step, carry):
        share_copy(step).start()
        return carry

    lax.fori_loop(0, SUPERS, start_share, 0)

    def share_step(step, carry):
        share_copy(step).wait_recv()
        rows = rows_of(block(step))
        high, low = split(fed[core, rows, :] + share_in[rows, :])
        shared[rows, :F] = high
        shared[rows, F:] = low
        return carry

    lax.fori_loop(0, SUPERS, share_step, 0)
    most = pl.ds(0, CHIPS - 1)
    pltpu.make_async_copy(ring_in.at[most], ring_in.at[most], ring_recv).wait()
    quad_in[quad] = jnp.sum(ring_in[...], axis=0)

    for i in (2, 1, 3):
        pltpu.make_async_remote_copy(
            src_ref=quad_in.at[quad], dst_ref=quad_in.at[quad], send_sem=quad_send, recv_sem=quad_recv,
            device_id=quads[i], device_id_type=MESH).start()
    three = pl.ds(0, QUADS - 1)
    pltpu.make_async_copy(quad_in.at[three], quad_in.at[three], quad_recv).wait()
    left[core, me] = (quad_in[0] + quad_in[1]) + (quad_in[2] + quad_in[3])

    def gather_copy(slot, target):
        return pltpu.make_async_remote_copy(
            src_ref=left.at[core, slot], dst_ref=left.at[core, slot], send_sem=gather_send,
            recv_sem=gather_recv.at[slot], device_id=target, device_id_type=MESH)

    for offset in OFFSETS:
        gather_copy(me, device_at(offset)).start()

    def pass_copy(step, side):
        at = slots_of(block(step))
        return pltpu.make_async_remote_copy(
            src_ref=left.at[side, at], dst_ref=left.at[side, at], send_sem=pass_send.at[step],
            recv_sem=pass_recv.at[step], device_id=partner, device_id_type=MESH)

    def left_block(m, b):
        high, low = split(jnp.concatenate([left[m, b * SUB + j] for j in range(SUB)], axis=1))
        return jnp.concatenate([high, low], axis=0)

    def gather(step, kept):
        b = block(step)
        for dy in (0, 1):
            for dz in (0, 1):
                if (dy, dz) != (0, 0) or not kept:
                    gather_copy(b * SUB + ((y + dy) & 1) * 2 + bits[dz], partner).wait_recv()
        pass_copy(step, core).start()
        acc[...] += nn(left_block(core, b), shared[rows_of(b), :])

    def gather_step(i, carry):
        gather(SUPERS - 1 - i, False)
        return carry

    acc[...] = jnp.zeros_like(acc)
    gather(SUPERS - 1, True)
    lax.fori_loop(1, SUPERS, gather_step, 0)

    t_plane[chip] = acc[:RANK, :F] + (acc[RANK:, :F] + acc[:RANK, F:]) + acc[RANK:, F:]
    for dx, dy, dz in OFFSETS:
        if dz == 0:
            pltpu.make_async_remote_copy(
                src_ref=t_plane.at[chip], dst_ref=t_plane.at[chip], send_sem=plane_send, recv_sem=plane_recv,
                device_id=device_at((dx, dy, 0)), device_id_type=MESH).start()

    def gram_step(b, total):
        both = left_block(core, b)
        return total + nt(both, both)

    products = lax.fori_loop(0, SUPERS, gram_step, jnp.zeros((2 * RANK, 2 * RANK), F32))
    gram = (products[:RANK, :RANK] + products[RANK:, RANK:]) + (products[:RANK, RANK:] + products[RANK:, :RANK])
    row = lax.broadcasted_iota(jnp.int32, (RANK, RANK), 0)
    column = lax.broadcasted_iota(jnp.int32, (RANK, RANK), 1)
    unit = jnp.where(row == column, 1.0, 0.0).astype(F32)
    work = jnp.concatenate([unit, gram, jnp.zeros((RANK, 2 * RANK), F32)], axis=1)
    wide_row = lax.broadcasted_iota(jnp.int32, (RANK, 4 * RANK), 0)
    wide_column = lax.broadcasted_iota(jnp.int32, (RANK, 4 * RANK), 1)
    pivots = jnp.ones((RANK, 1), F32)
    for j in range(RANK):
        picked = work[:, RANK + j : RANK + j + 1]
        pivot = picked[j : j + 1, :]
        pivots = jnp.where(wide_row[:, :1] == j, pivot, pivots)
        work = work - jnp.where(wide_row[:, :1] > j, picked / pivot, 0.0) * work[j : j + 1, :]
    inverse = jnp.where(wide_column < RANK, work * lax.rsqrt(pivots), 0.0)
    lower = jnp.concatenate([inverse, jnp.zeros((3 * RANK, 4 * RANK), F32)], axis=0)
    upper = lower.T

    def turn_step(step, carry):
        pass_copy(step, 1 - core).wait_recv()
        b = block(step)
        for j in range(SUB):
            slot = b * SUB + j
            key_high, key_low = split(left[0, slot])
            value_high, value_low = split(left[1, slot])
            both = jnp.concatenate(
                [piece.astype(F32) for piece in (key_high, value_high, key_low, value_low)], axis=0)
            left_rows[pl.ds(pl.multiple_of(slot * 128, 128), 128), :] = both.T.astype(BF16)
        return carry

    lax.fori_loop(0, SUPERS, turn_step, 0)

    fifteen = pl.ds(0, PLANE - 1)
    pltpu.make_async_copy(t_plane.at[fifteen], t_plane.at[fifteen], plane_recv).wait()
    sums = jnp.concatenate([jnp.sum(t_plane[...], axis=0), jnp.zeros((3 * RANK, F), F32)], axis=0) * (1.0 / 32)
    right = full(lower, sums)
    result[core, :RANK] = right[:RANK]
    result[core, RANK:] = full(upper, right)[:RANK]
    last = pltpu.make_async_remote_copy(
        src_ref=result.at[core], dst_ref=result.at[core], send_sem=last_send, recv_sem=last_recv,
        device_id=partner, device_id_type=MESH)
    last.start()

    def end_step(step, carry):
        pair_copy(step).wait_send()
        share_copy(step).wait_send()
        pass_copy(step, core).wait_send()
        return carry

    lax.fori_loop(0, SUPERS, end_step, 0)
    pltpu.make_async_copy(ring_in.at[most], ring_in.at[most], ring_send).wait()
    pltpu.make_async_copy(quad_in.at[three], quad_in.at[three], quad_send).wait()
    pltpu.make_async_copy(ring_in.at[most], ring_in.at[most], gather_send).wait()
    pltpu.make_async_copy(t_plane.at[fifteen], t_plane.at[fifteen], plane_send).wait()
    last.wait()


def error_kernel(fed, left_rows, result, right_key, right_value, new_key, new_value, wide, out, sem):
    right_key[...] = result[0, :RANK]
    right_value[...] = result[1, :RANK]
    wide[...] = jnp.zeros_like(wide)
    for m in range(2):
        for part_of, piece in enumerate(split(result[m, RANK:])):
            for again in range(2):
                row = (2 * part_of + again) * 2 * RANK + m * RANK
                wide[row : row + RANK, m * F : (m + 1) * F] = piece
    copies = []
    for b in range(SUPERS):
        rows = slice(b * ROWS, (b + 1) * ROWS)
        tall = left_rows[rows, :]
        change = nn(jnp.concatenate([tall, tall], axis=1), wide[...])
        for m, new in enumerate((new_key, new_value)):
            out[m, rows, :] = fed[m, rows, :] - change[:, m * F : (m + 1) * F]
            copy = pltpu.make_async_copy(out.at[m, rows], new.at[0, rows], sem.at[b, m])
            copy.start()
            copies.append(copy)
    for copy in copies:
        copy.wait()


def on_device(grad_key, grad_value, error_key, error_value, factor_key, factor_value):
    vmem = pl.BlockSpec(memory_space=pltpu.VMEM)
    anywhere = pl.BlockSpec(memory_space=pl.ANY)
    dma = pltpu.SemaphoreType.DMA
    fed, left_rows, result = pl.pallas_call(
        reduce_kernel,
        out_shape=(
            pltpu.VMEM((2, D, F), F32),
            pltpu.VMEM((D, 4 * RANK), BF16),
            pltpu.VMEM((2, 2 * RANK, F), F32),
        ),
        in_specs=[anywhere] * 6,
        out_specs=(vmem,) * 3,
        scratch_shapes=[
            pltpu.VMEM((4, D, F), F32),
            pltpu.VMEM((2, RANK, F), F32),
            pltpu.VMEM((4 * RANK, 2 * F), BF16),
            pltpu.VMEM((2, CHIPS, RANK, 128), F32),
            pltpu.VMEM((CHIPS, RANK, 128), F32),
            pltpu.VMEM((CHIPS, RANK, 128), F32),
            pltpu.VMEM((QUADS, RANK, 128), F32),
            pltpu.VMEM((2, CHIPS, RANK, 128), F32),
            pltpu.VMEM((D, F), F32),
            pltpu.VMEM((D, 2 * F), BF16),
            pltpu.VMEM((2 * RANK, 2 * F), F32),
            pltpu.VMEM((PLANE, RANK, F), F32),
            dma((2,)),
            dma((SUPERS, 4)),
            dma((SUPERS,)),
            dma((SUPERS,)),
            dma,
            dma,
            dma((SUPERS,)),
            dma((SUPERS,)),
            dma,
            dma,
            dma,
            dma((CHIPS,)),
            dma((SUPERS,)),
            dma((SUPERS,)),
            dma,
            dma,
            dma,
            dma,
        ],
        compiler_params=pltpu.CompilerParams(
            collective_id=0, has_side_effects=True, vmem_limit_bytes=32 * 2**20
        ),
        cost_estimate=pl.CostEstimate(flops=10**9, bytes_accessed=12 * 2**20, transcendentals=0),
        name="reduce_factors",
    )(*(pltpu.with_memory_space_constraint(a, pltpu.HBM) for a in (grad_key, grad_value, error_key, error_value, factor_key.T, factor_value.T)))
    right_key, right_value, new_key, new_value = pl.pallas_call(
        error_kernel,
        out_shape=(
            jax.ShapeDtypeStruct((RANK, F), F32),
            jax.ShapeDtypeStruct((RANK, F), F32),
            jax.ShapeDtypeStruct((1, D, F), F32),
            jax.ShapeDtypeStruct((1, D, F), F32),
        ),
        in_specs=[vmem] * 3,
        out_specs=(vmem, vmem, anywhere, anywhere),
        scratch_shapes=[
            pltpu.VMEM((8 * RANK, 2 * F), BF16),
            pltpu.VMEM((2, D, F), F32),
            dma((SUPERS, 2)),
        ],
        compiler_params=pltpu.CompilerParams(vmem_limit_bytes=32 * 2**20),
        cost_estimate=pl.CostEstimate(flops=10**9, bytes_accessed=8 * 2**20, transcendentals=0),
        name="new_errors",
    )(fed, left_rows, result)
    return right_key.T, right_value.T, new_key, new_value


def solution(mesh):
    in_specs = (
        P("dp", None, "tensor"),
        P("dp", None, "tensor"),
        P("dp", None, "tensor"),
        P("dp", None, "tensor"),
        P("tensor", None),
        P("tensor", None),
    )
    out_specs = (
        P("tensor", None),
        P("tensor", None),
        P("dp", None, "tensor"),
        P("dp", None, "tensor"),
    )
    return jax.shard_map(
        on_device, mesh=mesh, in_specs=in_specs, out_specs=out_specs, check_vma=False
    )
```

time: 63 us -> 48 us (0.76)
  local copies, waits for them, and re-layouts: 7.79 us -> 0 us
  Pallas kernels: 54.2 us -> 47.2 us
    unnamed x12 -> x0, local copies, waits for them, and re-layouts: 7.79 us -> none
    pallas_call x1, Pallas kernels: 51.2 us -> 44.1 us  [on_device(): pl.pallas_call(reduce_kernel, out_shape=(pltpu.VMEM((2, D, F), F32), pltp...]
where the time goes in v2:
time: 48 us; the launch traced here: 47.9 us
  Pallas kernels  47.2 us (98%)
  between operations  0.64 us (1%)
    pallas_call x1, Pallas kernels, on_device(): pl.pallas_call(reduce_kernel, out_shape=(pltpu.VMEM((2, D, F), F32), pltp...  44.1 us
    pallas_call x1, Pallas kernels, on_device(): pl.pallas_call(error_kernel, out_shape=(jax.ShapeDtypeStruct((RANK, F), F...  3.07 us

profile of v2, /device:TPU:1, one launch (start us, length us, event | category | flops | bytes accessed | tf_op | source)
XLA Modules:
  0.0 47.9 jit_solution(14302035276678011593)
XLA Ops:
  0.6 44.1 %reduce_factors.1 = (f32[2,4096,128]{2,1,0:T(8,128)S(1)}, bf16[4096,128]{1,0:T(8,128)(2,1)S(1)}, f32[2,64,128]{2,1,0:T(8,128)S(1)}) custom-call(f32[1,4096,128]{2,1,0:T(8,128)} %gk.1, f32[1,4096,128]{2,1,0:T(8,128)} %gv.1, f32[1,4096,128]{2,1,0:T(8,128)} %ek.1, f32[1,4096,128]{2,1,0:T(8,128)} %ev.1, f32[32,128]{1,0:T(8,128)} %bitcast.4, f32[32,128]{1,0:T(8,128)} %bitcast.5), custom_call_target="tpu_custom_call" | custom-call | flops 1000000000 | bytes 12582912 | tf_op jit(solution)/shard_map/reduce_factors/pallas_call | solution.py:332
  44.8 3.1 %new_errors.1 = (f32[32,128]{1,0:T(8,128)}, f32[32,128]{1,0:T(8,128)}, f32[1,4096,128]{2,1,0:T(8,128)}, f32[1,4096,128]{2,1,0:T(8,128)}) custom-call(f32[2,4096,128]{2,1,0:T(8,128)S(1)} %get-tuple-element.11.fed, bf16[4096,128]{1,0:T(8,128)(2,1)S(1)} %get-tuple-element.12.left_rows, f32[2,64,128]{2,1,0:T(8,128)S(1)} %get-tuple-element.13.result), custom_call_target="tpu_custom_call" | custom-call | flops 1000000000 | bytes 8388608 | tf_op jit(solution)/shard_map/new_errors/pallas_call | solution.py:379

commit v3 on v2

--- a/solution.py
+++ b/solution.py
@@ -16,13 +16,24 @@
 SUPERS = 8
 ROWS = D // SUPERS
 SUB = ROWS // 128
+AHEAD = 5
 CHIPS = 32
 PLANE = 16
 QUADS = 4
-OFFSETS = sorted(
-    [(dx, dy, dz) for dx in range(4) for dy in range(4) for dz in range(2) if dx + dy + dz > 0],
-    key=lambda o: -(min(o[0], 4 - o[0]) + min(o[1], 4 - o[1]) + o[2]),
-)
+
+
+def far_first():
+    offsets = [(dx, dy, dz) for dx in range(4) for dy in range(4) for dz in range(2) if dx + dy + dz > 0]
+    offsets.sort(key=lambda o: -(min(o[0], 4 - o[0]) + min(o[1], 4 - o[1]) + o[2]))
+    order = []
+    for dx, dy, dz in offsets:
+        for offset in ((dx, dy, dz), (-dx % 4, -dy % 4, dz)):
+            if offset not in order:
+                order.append(offset)
+    return order
+
+
+OFFSETS = far_first()
 
 
 def nt(a, b):
@@ -42,10 +53,31 @@
     return high, (value - high.astype(F32)).astype(BF16)
 
 
+def thirds(value):
+    high = value.astype(BF16)
+    rest = value - high.astype(F32)
+    mid = rest.astype(BF16)
+    return high, mid, (rest - mid.astype(F32)).astype(BF16)
+
+
+def tall_of(block):
+    high, low = split(block)
+    return jnp.concatenate([high.astype(F32), low.astype(F32)], axis=0).T.astype(BF16)
+
+
+def wide_of(weight):
+    high, low = split(weight)
+    return jnp.concatenate([high, high, low, low], axis=0)
+
+
+def low_rank(tall, wide):
+    return nn(tall, wide[: 2 * RANK, :]) + nn(tall, wide[2 * RANK :, :])
+
+
 def reduce_kernel(
     gk, gv, ek, ev, qk, qv,
-    fed, left_rows, result,
-    stage, q_in, q_all, part, pair_in, ring_in, quad_in, left, share_in, shared, acc, t_plane,
+    fed, left, result,
+    stage, q_in, q_all, part, pair_in, ring_in, quad_in, share_in, shared, acc, gram_acc, t_plane, left_rows, own, spread,
     q_sem, load_sem, pair_send, pair_recv, ring_send, ring_recv, share_send, share_recv, quad_send, quad_recv,
     gather_send, gather_recv, pass_send, pass_recv, plane_send, plane_recv, last_send, last_recv,
 ):
@@ -127,20 +159,11 @@
                 part[m, b * SUB + j] = total[m * RANK : (m + 1) * RANK, j * 128 : (j + 1) * 128]
         return carry
 
-    lax.fori_loop(0, SUPERS, add_left, 0)
-    pl.semaphore_wait(barrier, len(OFFSETS) + QUADS)
-
     def pair_copy(step):
         at = slots_of(block(step))
         return pltpu.make_async_remote_copy(
             src_ref=part.at[1 - core, at], dst_ref=pair_in.at[at], send_sem=pair_send.at[step],
             recv_sem=pair_recv.at[step], device_id=partner, device_id_type=MESH)
-
-    def start_pair(step, carry):
-        pair_copy(step).start()
-        return carry
-
-    lax.fori_loop(0, SUPERS, start_pair, 0)
 
     def ring_copy(member):
         target = ((member >> 1) * 2 + core, quad * 2 + (member & 1))
@@ -158,11 +181,26 @@
                 if (dy, dz) != (0, 0) or not kept:
                     ring_copy(b * SUB + ((y + dy) & 1) * 2 + bits[dz]).start()
 
+    def start_pair(step, carry):
+        pair_copy(step).start()
+        return carry
+
     def scatter_step(step, carry):
         scatter(step, False)
         return carry
 
-    lax.fori_loop(0, SUPERS - 1, scatter_step, 0)
+    def overlapped(step, carry):
+        add_left(step, 0)
+        pair_copy(step).start()
+        scatter(2 * (step - AHEAD), False)
+        scatter(2 * (step - AHEAD) + 1, False)
+        return carry
+
+    lax.fori_loop(0, AHEAD, add_left, 0)
+    pl.semaphore_wait(barrier, len(OFFSETS) + QUADS)
+    lax.fori_loop(0, AHEAD, start_pair, 0)
+    lax.fori_loop(AHEAD, SUPERS, overlapped, 0)
+    lax.fori_loop(2 * (SUPERS - AHEAD), SUPERS - 1, scatter_step, 0)
     scatter(SUPERS - 1, True)
     ring_in[me] = part[core, me]
 
@@ -223,16 +261,25 @@
             for dz in (0, 1):
                 if (dy, dz) != (0, 0) or not kept:
                     gather_copy(b * SUB + ((y + dy) & 1) * 2 + bits[dz], partner).wait_recv()
-        pass_copy(step, core).start()
         acc[...] += nn(left_block(core, b), shared[rows_of(b), :])
 
-    def gather_step(i, carry):
-        gather(SUPERS - 1 - i, False)
+    def digest(step):
+        b = block(step)
+        both = left_block(core, b)
+        gram_acc[...] += nt(both, both)
+        for j in range(SUB):
+            rows = pl.ds(pl.multiple_of((b * SUB + j) * 128, 128), 128)
+            left_rows[rows, : 2 * RANK] = tall_of(left[core, b * SUB + j])
+
+    def gather_step(step, carry):
+        gather(step, False)
         return carry
 
     acc[...] = jnp.zeros_like(acc)
+    gram_acc[...] = jnp.zeros_like(gram_acc)
+    gather(0, False)
+    lax.fori_loop(1, SUPERS - 1, gather_step, 0)
     gather(SUPERS - 1, True)
-    lax.fori_loop(1, SUPERS, gather_step, 0)
 
     t_plane[chip] = acc[:RANK, :F] + (acc[RANK:, :F] + acc[:RANK, F:]) + acc[RANK:, F:]
     for dx, dy, dz in OFFSETS:
@@ -241,11 +288,18 @@
                 src_ref=t_plane.at[chip], dst_ref=t_plane.at[chip], send_sem=plane_send, recv_sem=plane_recv,
                 device_id=device_at((dx, dy, 0)), device_id_type=MESH).start()
 
-    def gram_step(b, total):
-        both = left_block(core, b)
-        return total + nt(both, both)
-
-    products = lax.fori_loop(0, SUPERS, gram_step, jnp.zeros((2 * RANK, 2 * RANK), F32))
+    def start_pass(step, carry):
+        pass_copy(step, core).start()
+        return carry
+
+    lax.fori_loop(0, SUPERS, start_pass, 0)
+
+    def digest_step(step, carry):
+        digest(step)
+        return carry
+
+    lax.fori_loop(0, SUPERS, digest_step, 0)
+    products = gram_acc[...]
     gram = (products[:RANK, :RANK] + products[RANK:, RANK:]) + (products[:RANK, RANK:] + products[RANK:, :RANK])
     row = lax.broadcasted_iota(jnp.int32, (RANK, RANK), 0)
     column = lax.broadcasted_iota(jnp.int32, (RANK, RANK), 1)
@@ -259,39 +313,36 @@
         pivot = picked[j : j + 1, :]
         pivots = jnp.where(wide_row[:, :1] == j, pivot, pivots)
         work = work - jnp.where(wide_row[:, :1] > j, picked / pivot, 0.0) * work[j : j + 1, :]
-    inverse = jnp.where(wide_column < RANK, work * lax.rsqrt(pivots), 0.0)
-    lower = jnp.concatenate([inverse, jnp.zeros((3 * RANK, 4 * RANK), F32)], axis=0)
-    upper = lower.T
-
-    def turn_step(step, carry):
-        pass_copy(step, 1 - core).wait_recv()
-        b = block(step)
-        for j in range(SUB):
-            slot = b * SUB + j
-            key_high, key_low = split(left[0, slot])
-            value_high, value_low = split(left[1, slot])
-            both = jnp.concatenate(
-                [piece.astype(F32) for piece in (key_high, value_high, key_low, value_low)], axis=0)
-            left_rows[pl.ds(pl.multiple_of(slot * 128, 128), 128), :] = both.T.astype(BF16)
-        return carry
-
-    lax.fori_loop(0, SUPERS, turn_step, 0)
+    inverse = (work * lax.rsqrt(pivots))[:, :RANK]
+    square = jnp.concatenate([inverse, jnp.zeros((RANK, 3 * RANK), F32)], axis=1)
+    upper = jnp.concatenate([square, jnp.zeros((3 * RANK, 4 * RANK), F32)], axis=0).T
+    solver = jnp.concatenate([inverse, full(upper[:RANK, :RANK], inverse)], axis=0) * (1.0 / 32)
+    s_high, s_mid, s_low = thirds(solver)
+    spread[:, : 6 * RANK] = jnp.concatenate([s_high, s_high, s_mid, s_mid, s_high, s_low], axis=1)
 
     fifteen = pl.ds(0, PLANE - 1)
     pltpu.make_async_copy(t_plane.at[fifteen], t_plane.at[fifteen], plane_recv).wait()
-    sums = jnp.concatenate([jnp.sum(t_plane[...], axis=0), jnp.zeros((3 * RANK, F), F32)], axis=0) * (1.0 / 32)
-    right = full(lower, sums)
-    result[core, :RANK] = right[:RANK]
-    result[core, RANK:] = full(upper, right)[:RANK]
+    high, mid, low = thirds(jnp.sum(t_plane[...], axis=0))
+    result[core] = nn(spread[:, : 6 * RANK], jnp.concatenate([high, mid, high, mid, low, high], axis=0))
     last = pltpu.make_async_remote_copy(
         src_ref=result.at[core], dst_ref=result.at[core], send_sem=last_send, recv_sem=last_recv,
         device_id=partner, device_id_type=MESH)
     last.start()
 
+    own[...] = wide_of(result[core, RANK:])
+
+    def own_step(b, carry):
+        rows = rows_of(b)
+        fed[core, rows, :] = fed[core, rows, :] - low_rank(left_rows[rows, : 2 * RANK], own)
+        return carry
+
+    lax.fori_loop(0, SUPERS, own_step, 0)
+
     def end_step(step, carry):
         pair_copy(step).wait_send()
         share_copy(step).wait_send()
         pass_copy(step, core).wait_send()
+        pass_copy(step, 1 - core).wait_recv()
         return carry
 
     lax.fori_loop(0, SUPERS, end_step, 0)
@@ -302,38 +353,40 @@
     last.wait()
 
 
-def error_kernel(fed, left_rows, result, right_key, right_value, new_key, new_value, wide, out, sem):
-    right_key[...] = result[0, :RANK]
-    right_value[...] = result[1, :RANK]
-    wide[...] = jnp.zeros_like(wide)
+def error_kernel(fed, left, result, right_key, right_value, new_key, new_value, wide, out, sem):
+    core = lax.axis_index("dp") & 1
+    news = (new_key, new_value)
+
+    def write(m):
+        done = pltpu.make_async_copy(fed.at[1 - m], news[1 - m].at[0], sem.at[SUPERS])
+        done.start()
+        right_key[...] = result[0, :RANK]
+        right_value[...] = result[1, :RANK]
+        wide[...] = wide_of(result[m, RANK:])
+        copies = []
+        for b in range(SUPERS):
+            rows = slice(b * ROWS, (b + 1) * ROWS)
+            tall = jnp.concatenate([tall_of(left[m, b * SUB + j]) for j in range(SUB)], axis=0)
+            out[rows, :] = fed[m, rows, :] - low_rank(tall, wide)
+            copies.append(pltpu.make_async_copy(out.at[rows], news[m].at[0, rows], sem.at[b]))
+            copies[-1].start()
+        for copy in copies:
+            copy.wait()
+        done.wait()
+
     for m in range(2):
-        for part_of, piece in enumerate(split(result[m, RANK:])):
-            for again in range(2):
-                row = (2 * part_of + again) * 2 * RANK + m * RANK
-                wide[row : row + RANK, m * F : (m + 1) * F] = piece
-    copies = []
-    for b in range(SUPERS):
-        rows = slice(b * ROWS, (b + 1) * ROWS)
-        tall = left_rows[rows, :]
-        change = nn(jnp.concatenate([tall, tall], axis=1), wide[...])
-        for m, new in enumerate((new_key, new_value)):
-            out[m, rows, :] = fed[m, rows, :] - change[:, m * F : (m + 1) * F]
-            copy = pltpu.make_async_copy(out.at[m, rows], new.at[0, rows], sem.at[b, m])
-            copy.start()
-            copies.append(copy)
-    for copy in copies:
-        copy.wait()
+        pl.when(core == 1 - m)(functools.partial(write, m))
 
 
 def on_device(grad_key, grad_value, error_key, error_value, factor_key, factor_value):
     vmem = pl.BlockSpec(memory_space=pltpu.VMEM)
     anywhere = pl.BlockSpec(memory_space=pl.ANY)
     dma = pltpu.SemaphoreType.DMA
-    fed, left_rows, result = pl.pallas_call(
+    fed, left, result = pl.pallas_call(
         reduce_kernel,
         out_shape=(
             pltpu.VMEM((2, D, F), F32),
-            pltpu.VMEM((D, 4 * RANK), BF16),
+            pltpu.VMEM((2, CHIPS, RANK, 128), F32),
             pltpu.VMEM((2, 2 * RANK, F), F32),
         ),
         in_specs=[anywhere] * 6,
@@ -346,11 +399,14 @@
             pltpu.VMEM((CHIPS, RANK, 128), F32),
             pltpu.VMEM((CHIPS, RANK, 128), F32),
             pltpu.VMEM((QUADS, RANK, 128), F32),
-            pltpu.VMEM((2, CHIPS, RANK, 128), F32),
             pltpu.VMEM((D, F), F32),
             pltpu.VMEM((D, 2 * F), BF16),
             pltpu.VMEM((2 * RANK, 2 * F), F32),
+            pltpu.VMEM((2 * RANK, 2 * RANK), F32),
             pltpu.VMEM((PLANE, RANK, F), F32),
+            pltpu.VMEM((D, 4 * RANK), BF16),
+            pltpu.VMEM((4 * RANK, F), BF16),
+            pltpu.VMEM((2 * RANK, 8 * RANK), BF16),
             dma((2,)),
             dma((SUPERS, 4)),
             dma((SUPERS,)),
@@ -387,14 +443,14 @@
         in_specs=[vmem] * 3,
         out_specs=(vmem, vmem, anywhere, anywhere),
         scratch_shapes=[
-            pltpu.VMEM((8 * RANK, 2 * F), BF16),
-            pltpu.VMEM((2, D, F), F32),
-            dma((SUPERS, 2)),
+            pltpu.VMEM((4 * RANK, F), BF16),
+            pltpu.VMEM((D, F), F32),
+            dma((SUPERS + 1,)),
         ],
         compiler_params=pltpu.CompilerParams(vmem_limit_bytes=32 * 2**20),
         cost_estimate=pl.CostEstimate(flops=10**9, bytes_accessed=8 * 2**20, transcendentals=0),
         name="new_errors",
-    )(fed, left_rows, result)
+    )(fed, left, result)
     return right_key.T, right_value.T, new_key, new_value
 
 

time: 48 us -> 46.2 us (0.963)
  Pallas kernels: 47.2 us -> 45.4 us
    pallas_call x1, Pallas kernels: 44.1 us -> 42.7 us  [on_device(): pl.pallas_call(reduce_kernel, out_shape=(pltpu.VMEM((2, D, F), F32), pltp...]
where the time goes in v3:
time: 46.2 us; the launch traced here: 46 us
  Pallas kernels  45.4 us (98%)
  between operations  0.64 us (1%)
    pallas_call x1, Pallas kernels, on_device(): pl.pallas_call(reduce_kernel, out_shape=(pltpu.VMEM((2, D, F), F32), pltp...  42.7 us
    pallas_call x1, Pallas kernels, on_device(): pl.pallas_call(error_kernel, out_shape=(jax.ShapeDtypeStruct((RANK, F), F...  2.7 us

profile of v3, /device:TPU:1, one launch (start us, length us, event | category | flops | bytes accessed | tf_op | source)
XLA Modules:
  0.0 46.0 jit_solution(12276024820980976120)
XLA Ops:
  0.6 42.7 %reduce_factors.1 = (f32[2,4096,128]{2,1,0:T(8,128)S(1)}, f32[2,32,32,128]{3,2,1,0:T(8,128)S(1)}, f32[2,64,128]{2,1,0:T(8,128)S(1)}) custom-call(f32[1,4096,128]{2,1,0:T(8,128)} %gk.1, f32[1,4096,128]{2,1,0:T(8,128)} %gv.1, f32[1,4096,128]{2,1,0:T(8,128)} %ek.1, f32[1,4096,128]{2,1,0:T(8,128)} %ev.1, f32[32,128]{1,0:T(8,128)} %bitcast.4, f32[32,128]{1,0:T(8,128)} %bitcast.5), custom_call_target="tpu_custom_call" | custom-call | flops 1000000000 | bytes 12582912 | tf_op jit(solution)/shard_map/reduce_factors/pallas_call | solution.py:385
  43.3 2.7 %new_errors.1 = (f32[32,128]{1,0:T(8,128)}, f32[32,128]{1,0:T(8,128)}, f32[1,4096,128]{2,1,0:T(8,128)}, f32[1,4096,128]{2,1,0:T(8,128)}) custom-call(f32[2,4096,128]{2,1,0:T(8,128)S(1)} %get-tuple-element.11.fed, f32[2,32,32,128]{3,2,1,0:T(8,128)S(1)} %get-tuple-element.12.left, f32[2,64,128]{2,1,0:T(8,128)S(1)} %get-tuple-element.13.result), custom_call_target="tpu_custom_call" | custom-call | flops 1000000000 | bytes 8388608 | tf_op jit(solution)/shard_map/new_errors/pallas_call | solution.py:435

commit v4 on v3

--- a/solution.py
+++ b/solution.py
@@ -87,18 +87,19 @@
     chip = dp >> 1
     x = chip >> 2
     y = chip & 3
-    bit = z & 1
-    quad = z >> 1
+    shifted = (z + 8 - core) & 7
+    bit = shifted & 1
+    quad = shifted >> 1
     me = chip * 2 + bit
     xs = [(x + i) & 3 for i in range(4)]
     ys = [(y + i) & 3 for i in range(4)]
     bits = [bit, 1 - bit]
     partner = (chip * 2 + 1 - core, z)
-    quads = [(dp, ((quad + i) & 3) * 2 + bit) for i in range(QUADS)]
+    quads = [(dp, (z + 2 * i) & 7) for i in range(QUADS)]
 
     def device_at(offset):
         dx, dy, dz = offset
-        return ((xs[dx] * 4 + ys[dy]) * 2 + core, quad * 2 + bits[dz])
+        return ((xs[dx] * 4 + ys[dy]) * 2 + core, (quad * 2 + bits[dz] + core) & 7)
 
     def block(step):
         inner = (step >= 2) & (step < 6)
@@ -162,11 +163,11 @@
     def pair_copy(step):
         at = slots_of(block(step))
         return pltpu.make_async_remote_copy(
-            src_ref=part.at[1 - core, at], dst_ref=pair_in.at[at], send_sem=pair_send.at[step],
+            src_ref=part.at[1 - core, at], dst_ref=pair_in.at[at], send_sem=pair_send,
             recv_sem=pair_recv.at[step], device_id=partner, device_id_type=MESH)
 
     def ring_copy(member):
-        target = ((member >> 1) * 2 + core, quad * 2 + (member & 1))
+        target = ((member >> 1) * 2 + core, (quad * 2 + (member & 1) + core) & 7)
         return pltpu.make_async_remote_copy(
             src_ref=part.at[core, member], dst_ref=ring_in.at[me], send_sem=ring_send,
             recv_sem=ring_recv, device_id=target, device_id_type=MESH)
@@ -207,7 +208,7 @@
     def share_copy(step):
         rows = rows_of(block(step))
         return pltpu.make_async_remote_copy(
-            src_ref=fed.at[1 - core, rows], dst_ref=share_in.at[rows], send_sem=share_send.at[step],
+            src_ref=fed.at[1 - core, rows], dst_ref=share_in.at[rows], send_sem=share_send,
             recv_sem=share_recv.at[step], device_id=partner, device_id_type=MESH)
 
     def start_share(step, carry):
@@ -237,19 +238,16 @@
     pltpu.make_async_copy(quad_in.at[three], quad_in.at[three], quad_recv).wait()
     left[core, me] = (quad_in[0] + quad_in[1]) + (quad_in[2] + quad_in[3])
 
-    def gather_copy(slot, target):
-        return pltpu.make_async_remote_copy(
-            src_ref=left.at[core, slot], dst_ref=left.at[core, slot], send_sem=gather_send,
-            recv_sem=gather_recv.at[slot], device_id=target, device_id_type=MESH)
-
     for offset in OFFSETS:
-        gather_copy(me, device_at(offset)).start()
+        pltpu.make_async_remote_copy(
+            src_ref=left.at[core, me], dst_ref=left.at[core, me], send_sem=gather_send,
+            recv_sem=gather_recv.at[chip >> 1], device_id=device_at(offset), device_id_type=MESH).start()
 
     def pass_copy(step, side):
         at = slots_of(block(step))
         return pltpu.make_async_remote_copy(
-            src_ref=left.at[side, at], dst_ref=left.at[side, at], send_sem=pass_send.at[step],
-            recv_sem=pass_recv.at[step], device_id=partner, device_id_type=MESH)
+            src_ref=left.at[side, at], dst_ref=left.at[side, at], send_sem=pass_send,
+            recv_sem=pass_recv, device_id=partner, device_id_type=MESH)
 
     def left_block(m, b):
         high, low = split(jnp.concatenate([left[m, b * SUB + j] for j in range(SUB)], axis=1))
@@ -257,10 +255,8 @@
 
     def gather(step, kept):
         b = block(step)
-        for dy in (0, 1):
-            for dz in (0, 1):
-                if (dy, dz) != (0, 0) or not kept:
-                    gather_copy(b * SUB + ((y + dy) & 1) * 2 + bits[dz], partner).wait_recv()
+        arrived = left.at[core, pl.ds(b * SUB, SUB - 1 if kept else SUB)]
+        pltpu.make_async_copy(arrived, arrived, gather_recv.at[b]).wait()
         acc[...] += nn(left_block(core, b), shared[rows_of(b), :])
 
     def digest(step):
@@ -338,14 +334,8 @@
 
     lax.fori_loop(0, SUPERS, own_step, 0)
 
-    def end_step(step, carry):
-        pair_copy(step).wait_send()
-        share_copy(step).wait_send()
-        pass_copy(step, core).wait_send()
-        pass_copy(step, 1 - core).wait_recv()
-        return carry
-
-    lax.fori_loop(0, SUPERS, end_step, 0)
+    for ref, sem in ((pair_in, pair_send), (share_in, share_send), (ring_in, pass_send), (ring_in, pass_recv)):
+        pltpu.make_async_copy(ref, ref, sem).wait()
     pltpu.make_async_copy(ring_in.at[most], ring_in.at[most], ring_send).wait()
     pltpu.make_async_copy(quad_in.at[three], quad_in.at[three], quad_send).wait()
     pltpu.make_async_copy(ring_in.at[most], ring_in.at[most], gather_send).wait()
@@ -409,18 +399,18 @@
             pltpu.VMEM((2 * RANK, 8 * RANK), BF16),
             dma((2,)),
             dma((SUPERS, 4)),
+            dma,
             dma((SUPERS,)),
+            dma,
+            dma,
+            dma,
             dma((SUPERS,)),
             dma,
             dma,
+            dma,
             dma((SUPERS,)),
-            dma((SUPERS,)),
-            dma,
-            dma,
-            dma,
-            dma((CHIPS,)),
-            dma((SUPERS,)),
-            dma((SUPERS,)),
+            dma,
+            dma,
             dma,
             dma,
             dma,

time: 46.2 us -> 46 us (level)
  no operation moved by 1% of the time
where the time goes in v4:
time: 46 us; the launch traced here: 45.9 us
  Pallas kernels  45.2 us (98%)
  between operations  0.64 us (1%)
    pallas_call x1, Pallas kernels, on_device(): pl.pallas_call(reduce_kernel, out_shape=(pltpu.VMEM((2, D, F), F32), pltp...  42.5 us
    pallas_call x1, Pallas kernels, on_device(): pl.pallas_call(error_kernel, out_shape=(jax.ShapeDtypeStruct((RANK, F), F...  2.7 us

profile of v4, /device:TPU:1, one launch (start us, length us, event | category | flops | bytes accessed | tf_op | source)
XLA Modules:
  0.0 45.9 jit_solution(18083936412554402984)
XLA Ops:
  0.6 42.5 %reduce_factors.1 = (f32[2,4096,128]{2,1,0:T(8,128)S(1)}, f32[2,32,32,128]{3,2,1,0:T(8,128)S(1)}, f32[2,64,128]{2,1,0:T(8,128)S(1)}) custom-call(f32[1,4096,128]{2,1,0:T(8,128)} %gk.1, f32[1,4096,128]{2,1,0:T(8,128)} %gv.1, f32[1,4096,128]{2,1,0:T(8,128)} %ek.1, f32[1,4096,128]{2,1,0:T(8,128)} %ev.1, f32[32,128]{1,0:T(8,128)} %bitcast.4, f32[32,128]{1,0:T(8,128)} %bitcast.5), custom_call_target="tpu_custom_call" | custom-call | flops 1000000000 | bytes 12582912 | tf_op jit(solution)/shard_map/reduce_factors/pallas_call | solution.py:375
  43.2 2.7 %new_errors.1 = (f32[32,128]{1,0:T(8,128)}, f32[32,128]{1,0:T(8,128)}, f32[1,4096,128]{2,1,0:T(8,128)}, f32[1,4096,128]{2,1,0:T(8,128)}) custom-call(f32[2,4096,128]{2,1,0:T(8,128)S(1)} %get-tuple-element.11.fed, f32[2,32,32,128]{3,2,1,0:T(8,128)S(1)} %get-tuple-element.12.left, f32[2,64,128]{2,1,0:T(8,128)S(1)} %get-tuple-element.13.result), custom_call_target="tpu_custom_call" | custom-call | flops 1000000000 | bytes 8388608 | tf_op jit(solution)/shard_map/new_errors/pallas_call | solution.py:425

commit v5 on v4

--- a/solution.py
+++ b/solution.py
@@ -186,10 +186,6 @@
         pair_copy(step).start()
         return carry
 
-    def scatter_step(step, carry):
-        scatter(step, False)
-        return carry
-
     def overlapped(step, carry):
         add_left(step, 0)
         pair_copy(step).start()
@@ -199,9 +195,12 @@
 
     lax.fori_loop(0, AHEAD, add_left, 0)
     pl.semaphore_wait(barrier, len(OFFSETS) + QUADS)
-    lax.fori_loop(0, AHEAD, start_pair, 0)
-    lax.fori_loop(AHEAD, SUPERS, overlapped, 0)
-    lax.fori_loop(2 * (SUPERS - AHEAD), SUPERS - 1, scatter_step, 0)
+    for step in range(AHEAD):
+        start_pair(step, 0)
+    for step in range(AHEAD, SUPERS):
+        overlapped(step, 0)
+    for step in range(2 * (SUPERS - AHEAD), SUPERS - 1):
+        scatter(step, False)
     scatter(SUPERS - 1, True)
     ring_in[me] = part[core, me]
 
@@ -273,8 +272,8 @@
 
     acc[...] = jnp.zeros_like(acc)
     gram_acc[...] = jnp.zeros_like(gram_acc)
-    gather(0, False)
-    lax.fori_loop(1, SUPERS - 1, gather_step, 0)
+    for step in range(SUPERS - 1):
+        gather(step, False)
     gather(SUPERS - 1, True)
 
     t_plane[chip] = acc[:RANK, :F] + (acc[RANK:, :F] + acc[:RANK, F:]) + acc[RANK:, F:]

time: 46 us -> 45.3 us (0.985)
  Pallas kernels: 45.2 us -> 44.5 us
    pallas_call x1, Pallas kernels: 42.5 us -> 41.8 us  [on_device(): pl.pallas_call(reduce_kernel, out_shape=(pltpu.VMEM((2, D, F), F32), pltp...]
where the time goes in v5:
time: 45.3 us; the launch traced here: 45.1 us
  Pallas kernels  44.5 us (98%)
  between operations  0.64 us (1%)
    pallas_call x1, Pallas kernels, on_device(): pl.pallas_call(reduce_kernel, out_shape=(pltpu.VMEM((2, D, F), F32), pltp...  41.8 us
    pallas_call x1, Pallas kernels, on_device(): pl.pallas_call(error_kernel, out_shape=(jax.ShapeDtypeStruct((RANK, F), F...  2.7 us

profile of v5, /device:TPU:1, one launch (start us, length us, event | category | flops | bytes accessed | tf_op | source)
XLA Modules:
  0.0 45.1 jit_solution(9494083962798836456)
XLA Ops:
  0.6 41.8 %reduce_factors.1 = (f32[2,4096,128]{2,1,0:T(8,128)S(1)}, f32[2,32,32,128]{3,2,1,0:T(8,128)S(1)}, f32[2,64,128]{2,1,0:T(8,128)S(1)}) custom-call(f32[1,4096,128]{2,1,0:T(8,128)} %gk.1, f32[1,4096,128]{2,1,0:T(8,128)} %gv.1, f32[1,4096,128]{2,1,0:T(8,128)} %ek.1, f32[1,4096,128]{2,1,0:T(8,128)} %ev.1, f32[32,128]{1,0:T(8,128)} %bitcast.4, f32[32,128]{1,0:T(8,128)} %bitcast.5), custom_call_target="tpu_custom_call" | custom-call | flops 1000000000 | bytes 12582912 | tf_op jit(solution)/shard_map/reduce_factors/pallas_call | solution.py:374
  42.4 2.7 %new_errors.1 = (f32[32,128]{1,0:T(8,128)}, f32[32,128]{1,0:T(8,128)}, f32[1,4096,128]{2,1,0:T(8,128)}, f32[1,4096,128]{2,1,0:T(8,128)}) custom-call(f32[2,4096,128]{2,1,0:T(8,128)S(1)} %get-tuple-element.11.fed, f32[2,32,32,128]{3,2,1,0:T(8,128)S(1)} %get-tuple-element.12.left, f32[2,64,128]{2,1,0:T(8,128)S(1)} %get-tuple-element.13.result), custom_call_target="tpu_custom_call" | custom-call | flops 1000000000 | bytes 8388608 | tf_op jit(solution)/shard_map/new_errors/pallas_call | solution.py:424

commit v6 on v5

--- a/solution.py
+++ b/solution.py
@@ -170,7 +170,7 @@
         target = ((member >> 1) * 2 + core, (quad * 2 + (member & 1) + core) & 7)
         return pltpu.make_async_remote_copy(
             src_ref=part.at[core, member], dst_ref=ring_in.at[me], send_sem=ring_send,
-            recv_sem=ring_recv, device_id=target, device_id_type=MESH)
+            recv_sem=ring_recv.at[chip >> 1], device_id=target, device_id_type=MESH)
 
     def scatter(step, kept):
         pair_copy(step).wait_recv()
@@ -226,8 +226,13 @@
 
     lax.fori_loop(0, SUPERS, share_step, 0)
     most = pl.ds(0, CHIPS - 1)
-    pltpu.make_async_copy(ring_in.at[most], ring_in.at[most], ring_recv).wait()
-    quad_in[quad] = jnp.sum(ring_in[...], axis=0)
+    total = jnp.zeros((RANK, 128), F32)
+    for step in range(SUPERS):
+        b = block(step)
+        arrived = ring_in.at[pl.ds(b * SUB, SUB if step < SUPERS - 1 else SUB - 1)]
+        pltpu.make_async_copy(arrived, arrived, ring_recv.at[b]).wait()
+        total = total + jnp.sum(ring_in[slots_of(b)], axis=0)
+    quad_in[quad] = total
 
     for i in (2, 1, 3):
         pltpu.make_async_remote_copy(
@@ -401,7 +406,7 @@
             dma,
             dma((SUPERS,)),
             dma,
-            dma,
+            dma((SUPERS,)),
             dma,
             dma((SUPERS,)),
             dma,

time: 45.3 us -> 45.3 us (level)
  no operation moved by 1% of the time
where the time goes in v6:
time: 45.3 us; the launch traced here: 45.2 us
  Pallas kernels  44.5 us (98%)
  between operations  0.64 us (1%)
    pallas_call x1, Pallas kernels, on_device(): pl.pallas_call(reduce_kernel, out_shape=(pltpu.VMEM((2, D, F), F32), pltp...  41.8 us
    pallas_call x1, Pallas kernels, on_device(): pl.pallas_call(error_kernel, out_shape=(jax.ShapeDtypeStruct((RANK, F), F...  2.7 us

profile of v6, /device:TPU:1, one launch (start us, length us, event | category | flops | bytes accessed | tf_op | source)
XLA Modules:
  0.0 45.2 jit_solution(16772395299851916965)
XLA Ops:
  0.6 41.8 %reduce_factors.1 = (f32[2,4096,128]{2,1,0:T(8,128)S(1)}, f32[2,32,32,128]{3,2,1,0:T(8,128)S(1)}, f32[2,64,128]{2,1,0:T(8,128)S(1)}) custom-call(f32[1,4096,128]{2,1,0:T(8,128)} %gk.1, f32[1,4096,128]{2,1,0:T(8,128)} %gv.1, f32[1,4096,128]{2,1,0:T(8,128)} %ek.1, f32[1,4096,128]{2,1,0:T(8,128)} %ev.1, f32[32,128]{1,0:T(8,128)} %bitcast.4, f32[32,128]{1,0:T(8,128)} %bitcast.5), custom_call_target="tpu_custom_call" | custom-call | flops 1000000000 | bytes 12582912 | tf_op jit(solution)/shard_map/reduce_factors/pallas_call | solution.py:379
  42.5 2.7 %new_errors.1 = (f32[32,128]{1,0:T(8,128)}, f32[32,128]{1,0:T(8,128)}, f32[1,4096,128]{2,1,0:T(8,128)}, f32[1,4096,128]{2,1,0:T(8,128)}) custom-call(f32[2,4096,128]{2,1,0:T(8,128)S(1)} %get-tuple-element.11.fed, f32[2,32,32,128]{3,2,1,0:T(8,128)S(1)} %get-tuple-element.12.left, f32[2,64,128]{2,1,0:T(8,128)S(1)} %get-tuple-element.13.result), custom_call_target="tpu_custom_call" | custom-call | flops 1000000000 | bytes 8388608 | tf_op jit(solution)/shard_map/new_errors/pallas_call | solution.py:429
